TPU v7x, 32 devices: a whole 2x2x4 slice. The times are simulated.
32 devices in a mesh: groups: 2 (over y), node: 4 (over z), tensor: 4 (over x, core).
Axes of the slice: x: 2, y: 2, z: 4, core: 2. Of those that a mesh axis runs over, the one named last changes fastest.
Arguments:
- queries: bfloat16 [6144, 5120], P(('groups', 'node'), 'tensor'), parts along dimension 0, may hold values from -90 to 90
- keys: bfloat16 [6144, 1024], P(('groups', 'node'), 'tensor'), parts along dimension 0, may hold values from -4.1 to 4.1
- values: bfloat16 [6144, 1024], P(('groups', 'node'), 'tensor'), parts along dimension 0, may hold values from -4 to 4
- out_weight: bfloat16 [5120, 5120], P('node', 'tensor'), may hold values from -0.59765625 to 0.59765625
- slot_nodes: int32 [48], P('groups'), parts along dimension 0, may hold values from 0 to 23, as said below
- ancestors: int32 [48, 7], P('groups'), parts along dimension 0, may hold values from -1 to 23, as said below
- depth: int32 [48], P('groups'), parts along dimension 0, may hold values from 0 to 7, as said below
Outputs:
- projected: bfloat16 [6144, 5120], P(('groups', 'node', 'tensor')), parts along dimension 0
There are 2 independent parts, one for each index of `groups`. A program takes and returns all parts, laid end to end along the dimension named above; an argument that names none is the same for every part. Nothing has to cross between parts.
Inputs may be any that keep to these rules, and one draw needn't show every extreme that they name: `slot_nodes`: every node is held in exactly one slot. `ancestors`: every device holds one subtree: a node whose parent, if any, lies on another device, and its 5 children. When a node's parent lies on another device, that parent is one of the children of its device's subtree, and all nodes of other devices below a device hang below the same one of its children. Above any device lie at most 3 other devices. depth counts the entries of a row of ancestors that are not -1.
All inputs are finite; a program needn't handle non-finite values.
Results may differ from a plain program's by a relative error of at most 0.009.
Values may be sent and summed in bfloat16 or wider, within the bound.
No kernel may reach another device: no remote copies, remote signals or barrier semaphores. Data moves between devices by JAX's collectives and lax.ppermute only.
A program may use at most 128 MiB of HBM per device.

v0:
```python
import functools
import math

import jax
import jax.numpy as jnp
from jax import lax
from jax.experimental import pallas as pl
from jax.experimental.pallas import tpu as pltpu
from jax.sharding import PartitionSpec as P

HEAD = 128
NODE_TOK = 128
A_MAX = 7
CHAIN = A_MAX - 1
EXPORTS = 2
SCALE = math.log2(math.e) / math.sqrt(HEAD)
DEAD = -1e30
LIGHT = pl.CostEstimate(flops=1, bytes_accessed=1, transcendentals=0)
VMEM_LIMIT = 20 * 1024 * 1024
ATTEND_LIMIT = 56 * 1024 * 1024


def prepare_body(nodes, *refs):
    slot_hbm, ancestors_hbm, depth_hbm, keys, values, exported, table_hbm = refs[:7]
    slot_nodes, ancestors, depth, table, holder, within, roots, sem = refs[7:]
    devices = slot_nodes.shape[0] // nodes
    me = lax.axis_index("node")
    fetches = [
        pltpu.make_async_copy(source, target, sem.at[2 * EXPORTS + 1 + order])
        for order, (source, target) in enumerate(
            ((slot_hbm, slot_nodes), (ancestors_hbm, ancestors), (depth_hbm, depth))
        )
    ]
    for fetch in fetches:
        fetch.start()
    for fetch in fetches:
        fetch.wait()

    def place(device, mine):
        root, root_index = jnp.int32(0), jnp.int32(0)
        for index in range(nodes):
            node = slot_nodes[device * nodes + index]
            holder[node] = device
            within[node] = index
            even = (depth[node] & 1) == 0
            root = jnp.where(even, node, root)
            root_index = jnp.where(even, index, root_index)
        roots[device] = root
        return jnp.where(device == me, root_index, mine)

    root = lax.fori_loop(0, devices, place, jnp.int32(0))

    def find_attach(device, attach):
        node = roots[device]
        level = depth[node]
        for step in range(0, CHAIN, 2):
            above = jnp.maximum(ancestors[step, node], 0)
            hit = (step < level) & (holder[above] == me)
            attach = jnp.where(hit, within[above], attach)
        return attach

    attach = lax.fori_loop(0, devices, find_attach, jnp.int32(0))
    copies = []
    for position, (source, index) in enumerate(
        ((keys, root), (keys, attach), (values, root), (values, attach))
    ):
        rows = pl.ds(pl.multiple_of(index * NODE_TOK, NODE_TOK), NODE_TOK)
        copies.append(
            pltpu.make_async_copy(source.at[rows, :], exported.at[position], sem.at[position])
        )
    for copy in copies:
        copy.start()
    root_node = roots[me]
    count = depth[root_node]
    table[0] = root
    table[1] = count
    for step in range(CHAIN):
        above = jnp.maximum(ancestors[step, root_node], 0)
        entry = holder[above] * (2 * EXPORTS) + (1 if step % 2 == 0 else 0)
        table[2 + step] = jnp.where(step < count, entry, 0)
    store = pltpu.make_async_copy(table, table_hbm, sem.at[2 * EXPORTS])
    store.start()
    for copy in (*copies, store):
        copy.wait()


def prepare(slot_nodes, ancestors, depth, keys, values):
    nodes = keys.shape[0] // NODE_TOK
    slots = slot_nodes.shape[0]
    hbm = pl.BlockSpec(memory_space=pltpu.HBM)
    vmem = pl.BlockSpec(memory_space=pltpu.VMEM)
    return pl.pallas_call(
        functools.partial(prepare_body, nodes),
        out_shape=(
            jax.ShapeDtypeStruct((2 * EXPORTS, NODE_TOK, keys.shape[1]), keys.dtype),
            jax.ShapeDtypeStruct((2 + CHAIN,), jnp.int32),
        ),
        in_specs=[hbm, hbm, hbm, vmem, vmem],
        out_specs=(hbm, hbm),
        scratch_shapes=[
            pltpu.SMEM((slots,), jnp.int32),
            pltpu.SMEM((A_MAX, slots), jnp.int32),
            pltpu.SMEM((slots,), jnp.int32),
            pltpu.SMEM((2 + CHAIN,), jnp.int32),
            pltpu.SMEM((slots,), jnp.int32),
            pltpu.SMEM((slots,), jnp.int32),
            pltpu.SMEM((slots // nodes,), jnp.int32),
            pltpu.SemaphoreType.DMA((2 * EXPORTS + 4,)),
        ],
        compiler_params=pltpu.CompilerParams(vmem_limit_bytes=VMEM_LIMIT),
        name="prepare",
    )(slot_nodes, ancestors.T, depth, keys, values)


def attend_body(kv, parts, table, query_hbm, keys_hbm, values_hbm, got, *refs):
    out, query, keys, values, above_keys, above_values, all_keys, all_values, sem = refs[-9:]
    nodes = query.shape[0] // NODE_TOK
    group = query.shape[1] // HEAD
    per_part = query.shape[0] // parts
    side = all_keys.shape[0]
    lanes = pl.ds(kv * HEAD, HEAD)
    pairs = [(keys_hbm.at[:, lanes], keys), (values_hbm.at[:, lanes], values)]
    for step in range(CHAIN):
        entry = table[2 + step]
        pairs.append((got.at[entry, :, lanes], above_keys.at[step]))
        pairs.append((got.at[entry + EXPORTS, :, lanes], above_values.at[step]))
    pairs.append((query_hbm.at[:, pl.ds(kv * group * HEAD, group * HEAD)], query))
    copies = [
        pltpu.make_async_copy(source, target, sem.at[order])
        for order, (source, target) in enumerate(pairs)
    ]
    for copy in copies:
        copy.start()
    ones = jnp.ones((NODE_TOK, HEAD), all_values.dtype)
    nothing = jnp.zeros((NODE_TOK, 2 * HEAD), all_values.dtype)
    query_index = lax.broadcasted_iota(jnp.int32, (NODE_TOK, NODE_TOK), 0)
    key_index = lax.broadcasted_iota(jnp.int32, (NODE_TOK, NODE_TOK), 1)
    own_bias = jnp.where(key_index <= query_index, 0.0, DEAD)
    piece = math.gcd(NODE_TOK, per_part)
    pieces_part = per_part // piece
    me = lax.axis_index("tensor")
    above = (CHAIN + 1) * NODE_TOK
    for copy in copies:
        copy.wait()

    def node_rows(node):
        return pl.ds(pl.multiple_of(node * NODE_TOK, NODE_TOK), NODE_TOK)

    def put(place, order, key_block, value_block):
        rows = pl.ds(order * NODE_TOK, NODE_TOK)
        all_keys[place, rows, :] = key_block
        all_values[place, rows, :HEAD] = value_block
        all_values[place, rows, HEAD:] = ones

    def put_nothing(place, order, first_key):
        rows = pl.ds(order * NODE_TOK, NODE_TOK)
        all_keys[place, rows, :] = jnp.broadcast_to(first_key, (NODE_TOK, HEAD))
        all_values[place, rows, :] = nothing

    for place in range(side):
        for step in range(CHAIN):
            put(place, step, above_keys[step], above_values[step])

    def lay_out(place, node):
        own_key = keys[node_rows(node), :]
        put(place, CHAIN + 1, own_key, values[node_rows(node), :])
        for step in range(CHAIN):
            pl.when(step >= table[1])(functools.partial(put_nothing, place, step, own_key[:1]))
        is_root = node == table[0]
        pl.when(is_root)(functools.partial(put_nothing, place, CHAIN, own_key[:1]))

        @pl.when(jnp.logical_not(is_root))
        def _():
            put(place, CHAIN, keys[node_rows(table[0]), :], values[node_rows(table[0]), :])

    def score(place, node):
        stacked = jnp.concatenate(
            [query[node_rows(node), h * HEAD : (h + 1) * HEAD] for h in range(group)], 0
        )
        return times(stacked, all_keys[place])

    def weigh(scores):
        own = scores[:, above:] + jnp.concatenate([own_bias] * group, 0)
        masked = jnp.concatenate([scores[:, :above], own], 1)
        largest = jnp.max(masked, axis=1, keepdims=True)
        return jnp.exp2((masked - largest) * SCALE).astype(jnp.bfloat16)

    def finish(place, node, expo):
        mixed = jnp.dot(expo, all_values[place], preferred_element_type=jnp.float32)
        result = (mixed[:, :HEAD] / mixed[:, HEAD:]).astype(jnp.bfloat16)
        for part in range(NODE_TOK // piece):
            block = node * (NODE_TOK // piece) + part
            owner = block // pieces_part
            target = slot_position(parts, owner ^ me)
            inner = (block - owner * pieces_part) * piece
            to = pl.ds(pl.multiple_of(inner, piece), piece)
            for h in range(group):
                first = h * NODE_TOK + part * piece
                out[target, to, h * HEAD : (h + 1) * HEAD] = result[first : first + piece]

    def some_nodes(turn, carry):
        mine = [(place, turn * side + place) for place in range(side)]
        for place, node in mine:
            lay_out(place, node)
        scores = [score(place, node) for place, node in mine]
        for (place, node), each in zip(mine, scores):
            finish(place, node, weigh(each))
        return carry

    lax.fori_loop(0, nodes // side, some_nodes, 0)


def slot_position(parts, distance):
    half = parts // 2
    return jnp.where(distance % 2 == 1, distance // 2, half + distance // 2)


def attend(kv, table, queries, keys, values, got, parts, after):
    rows = queries.shape[0]
    width = queries.shape[1] // (keys.shape[1] // HEAD)
    total = (CHAIN + 2) * NODE_TOK
    side = 2 if rows % (2 * NODE_TOK) == 0 else 1
    hbm = pl.BlockSpec(memory_space=pltpu.HBM)
    return pl.pallas_call(
        functools.partial(attend_body, kv, parts),
        out_shape=jax.ShapeDtypeStruct((parts, rows // parts, width), queries.dtype),
        in_specs=[pl.BlockSpec(memory_space=pltpu.SMEM)]
        + [hbm] * 4
        + [pl.BlockSpec(memory_space=pl.ANY)] * len(after),
        scratch_shapes=[
            pltpu.VMEM((rows, width), queries.dtype),
            pltpu.VMEM((rows, HEAD), keys.dtype),
            pltpu.VMEM((rows, HEAD), keys.dtype),
            pltpu.VMEM((CHAIN, NODE_TOK, HEAD), keys.dtype),
            pltpu.VMEM((CHAIN, NODE_TOK, HEAD), keys.dtype),
            pltpu.VMEM((side, total, HEAD), keys.dtype),
            pltpu.VMEM((side, total, 2 * HEAD), keys.dtype),
            pltpu.SemaphoreType.DMA((3 + 2 * CHAIN,)),
        ],
        compiler_params=pltpu.CompilerParams(vmem_limit_bytes=ATTEND_LIMIT),
        cost_estimate=LIGHT,
        name="attend",
    )(table, queries, keys, values, got, *after)


def swap(array, axis, distance):
    size = lax.axis_size(axis)
    return lax.ppermute(array, axis, [(i, i ^ distance) for i in range(size)])


def times(rows, weight):
    return lax.dot_general(
        rows, weight, (((1,), (1,)), ((), ())), preferred_element_type=jnp.float32
    )


def is_middle(index):
    return (index == 1) | (index == 2)


def product(parts, pieces, sent, kept):
    half = parts[0].shape[0] // 2
    for out, start in ((sent, 0), (kept, half)):
        whole = jnp.concatenate([part[start : start + half, :] for part in parts], 1)
        column = 0
        for weight, first, count in pieces:
            out[:, column : column + count] = times(
                whole, weight[first : first + count, :]
            ).astype(out.dtype)
            column += count


def core_sum(pair, upper):
    kept, from_core = pair
    half = kept.shape[0] // 2
    rows = slice(half, 2 * half) if upper else slice(0, half)
    return kept[rows, :].astype(jnp.float32) + from_core[rows, :].astype(jnp.float32)


def step_body(plan, *refs):
    refs = list(refs)

    def take(count):
        return [refs.pop(0) for _ in range(count)]

    rows = [take(count) for count in plan["rows"]]
    arrays = take(plan["arrays"])
    weights = [
        [[(arrays[index], first, count) for index, first, count in pieces] for pieces in weight]
        for weight in plan["weights"]
    ]
    cores = [[take(2) for _ in range(count)] for count in plan["cores"]]
    chips = [([take(2) for _ in range(count)], take(1)[0]) for count in plan["chips"]]
    take(plan["after"])
    outs = take(plan["outs"])
    middle = is_middle(lax.axis_index("node"))
    picks = (middle, jnp.logical_not(middle))
    fetched = None
    for order, weight in enumerate(weights):
        if len(weight) == 2 and not plan["direct"]:
            chosen, sem = refs
            fetched = order
            for pick, pieces in zip(picks, weight):
                column = 0
                for array, first, count in pieces:
                    source = array.at[pl.ds(first, count), :]
                    target = chosen.at[pl.ds(column, count), :]
                    pl.when(pick)(pltpu.make_async_copy(source, target, sem).start)
                    column += count
    made = [[(outs.pop(0), outs.pop(0)) for _ in rows] for _ in weights]
    if plan["hold"]:
        for part in [x for parts in rows for x in parts]:
            out = outs.pop(0)
            out[...] = part[...]
    for bundle in cores:
        out, column = outs.pop(0), 0
        for pair in bundle:
            width = pair[0].shape[1]
            out[:, column : column + width] = core_sum(pair, True).astype(out.dtype)
            column += width
    for bundle, from_chip in chips:
        column = 0
        for pair in bundle:
            out = outs.pop(0)
            width = out.shape[1]
            away = from_chip[:, column : column + width].astype(jnp.float32)
            out[...] = (core_sum(pair, False) + away).astype(out.dtype)
            column += width
    for order, (weight, pairs) in enumerate(zip(weights, made)):
        if order == fetched:
            pltpu.make_async_copy(chosen, chosen, sem).wait()
            weight = [[(chosen, 0, chosen.shape[0])]]
        for parts, (sent, kept) in zip(rows, pairs):
            if len(weight) == 2:
                for pick, pieces in zip(picks, weight):
                    pl.when(pick)(functools.partial(product, parts, pieces, sent, kept))
            else:
                product(parts, weight[0], sent, kept)


def step(rows=(), weights=(), cores=(), chips=(), after=(), hold=False, direct=False):
    weights = [weight if isinstance(weight, tuple) else (weight,) for weight in weights]
    arrays, fetch, plans = [], [], []
    for weight in weights:
        plans.append([])
        for pieces in weight:
            plans[-1].append([])
            for array, first, count in pieces:
                known = [index for index, x in enumerate(arrays) if x is array]
                if not known:
                    known = [len(arrays)]
                    arrays.append(array)
                    fetch.append(len(weight) == 2 and not direct)
                plans[-1][-1].append((known[0], first, count))
    widths = [sum(count for _, _, count in weight[0]) for weight in weights]
    shapes = []
    for width in widths:
        shapes += [(parts[0].shape[0] // 2, width) for parts in rows for _ in range(2)]
    if hold:
        shapes += [part.shape for parts in rows for part in parts]
    for bundle in cores:
        shapes.append((bundle[0][0].shape[0] // 2, sum(kept.shape[1] for kept, _ in bundle)))
    for bundle in chips:
        shapes += [(kept.shape[0] // 2, kept.shape[1]) for kept, _ in bundle[:-1]]
    plan = {
        "rows": [len(parts) for parts in rows],
        "arrays": len(arrays),
        "weights": plans,
        "cores": [len(bundle) for bundle in cores],
        "chips": [len(bundle) - 1 for bundle in chips],
        "after": len(after),
        "outs": len(shapes),
        "hold": hold,
        "direct": direct,
    }
    vmem, hbm = pl.BlockSpec(memory_space=pltpu.VMEM), pl.BlockSpec(memory_space=pl.ANY)
    read = [(part, vmem) for parts in rows for part in parts]
    read += [(array, hbm if far else vmem) for array, far in zip(arrays, fetch)]
    read += [(x, vmem) for bundle in cores for pair in bundle for x in pair]
    for bundle in chips:
        read += [(x, vmem) for pair in bundle[:-1] for x in pair] + [(bundle[-1], vmem)]
    read += [(x, hbm) for x in after]
    dtype = read[0][0].dtype
    scratch = []
    if any(fetch):
        width = [w for w, weight in zip(widths, weights) if len(weight) == 2][0]
        scratch = [
            pltpu.VMEM((width, rows[0][0].shape[1] * len(rows[0])), dtype),
            pltpu.SemaphoreType.DMA,
        ]
    return pl.pallas_call(
        functools.partial(step_body, plan),
        out_shape=[jax.ShapeDtypeStruct(shape, dtype) for shape in shapes],
        in_specs=[spec for _, spec in read],
        scratch_shapes=scratch,
        compiler_params=pltpu.CompilerParams(vmem_limit_bytes=VMEM_LIMIT),
        cost_estimate=LIGHT,
        name="step",
    )(*[x for x, _ in read])


PAIRS = [(0, 1), (1, 0), (2, 3), (3, 2)]
MIDDLE = [(1, 2), (2, 1)]
OUTWARD = [(1, 0), (2, 3)]


def relay(piece, exported):
    near = lax.ppermute(piece, "node", PAIRS)
    across = lax.ppermute(piece, "node", MIDDLE)
    near, across, exported = lax.optimization_barrier((near, across, exported))
    across_out = lax.ppermute(across, "node", OUTWARD)
    near_across = lax.ppermute(near, "node", MIDDLE)
    return near, across, near_across, across_out


def place_body(spots, features, *refs):
    out = refs[-1]
    half = features // 2
    device = lax.axis_index("node")
    mine = lax.axis_index("groups")
    for source, (distance, side) in zip(refs[:-1], spots):
        group = {"own": mine, "other": 1 - mine, "first": 0, "second": 1}[side]
        column = pl.multiple_of((device ^ distance) * features + group * half, HEAD)
        out[:, pl.ds(column, source.shape[1])] = source[...]


def place(sources, spots, devices, features):
    return pl.pallas_call(
        functools.partial(place_body, spots, features),
        out_shape=jax.ShapeDtypeStruct(
            (sources[0].shape[0], devices * features), sources[0].dtype
        ),
        compiler_params=pltpu.CompilerParams(vmem_limit_bytes=VMEM_LIMIT),
        name="place",
    )(*sources)


def cut(weight):
    half = weight.shape[0] // 2
    return lax.dynamic_slice_in_dim(weight, lax.axis_index("groups") * half, half, 0)


def project_split(halves, relayed, out_weight):
    features = out_weight.shape[0]
    half = features // 2
    rows = [part.reshape(-1, part.shape[-1]) for part in halves]
    other = [swap(part, "groups", 1) for part in rows]
    near, across, near_across, across_out = relayed
    far_out = lax.ppermute(near_across, "node", OUTWARD)

    def core(sent):
        return swap(sent, "tensor", 1)

    def chip(away):
        return swap(away, "tensor", 2)

    def back(done):
        return swap(done, "groups", 1)

    def whole(weight):
        return [(weight, 0, weight.shape[0])]

    second = (whole(near_across), whole(across_out))
    far = (whole(across), whole(far_out))

    sent_a, kept_a, sent_b, kept_b, *rows = step(
        [rows], [[(out_weight, 0, half)], [(out_weight, half, half)]], hold=True
    )
    one = [(kept_a, core(sent_a))]
    (away,) = step(cores=[one])
    one.append(chip(away))
    sent_1, kept_1 = step([rows], [whole(near)], after=[away, other[0]])
    sent_2, kept_2, done_a = step([rows], [second], chips=[one], after=[sent_1])
    two = [(kept_b, core(sent_b)), (kept_1, core(sent_1)), (kept_2, core(sent_2))]
    (away,) = step(cores=[two])
    two.append(chip(away))
    sent_3, kept_3, sent_4, kept_4, *other = step(
        [other], [whole(near), second], after=[away], hold=True
    )
    three, four = [(kept_3, core(sent_3))], [(kept_4, core(sent_4))]
    away, done_b, done_1, done_2 = step(cores=[three], chips=[two])
    three.append(chip(away))
    away, done_3 = step(cores=[four], chips=[three])
    four.append(chip(away))
    back_3 = back(done_3)
    sent_5, kept_5 = step([other], [far], after=[away], direct=True)
    five = [(kept_5, core(sent_5))]
    (done_4,) = step(chips=[four], after=[sent_5, back_3])
    back_4 = back(done_4)
    sent_6, kept_6 = step([rows], [far], after=[done_4], direct=True)
    six = [(kept_6, core(sent_6))]
    (away,) = step(cores=[five], after=[sent_6])
    five.append(chip(away))
    (away,) = step(cores=[six], after=[away])
    six.append(chip(away))
    (done_5,) = step(chips=[five], after=[away, back_4])
    back_5 = back(done_5)
    (done_6,) = step(chips=[six], after=[done_5])
    return place(
        (done_a, done_b, done_1, done_2, back_3, back_4, back_5, done_6),
        (
            (0, "first"),
            (0, "second"),
            (1, "own"),
            (2, "own"),
            (1, "other"),
            (2, "other"),
            (3, "other"),
            (3, "own"),
        ),
        lax.axis_size("node"),
        features,
    )


def project_plain(halves, out_weight):
    attended = jnp.concatenate(halves, 2)
    parts, per_part, width = attended.shape
    me = lax.axis_index("tensor")
    order = slot_position(parts, jnp.arange(parts, dtype=jnp.int32) ^ me)
    rows = attended[order].reshape(parts * per_part, width)
    weight = lax.all_gather(out_weight, "node", axis=0, tiled=True)
    terms = times(rows, weight).astype(jnp.bfloat16)
    return lax.psum_scatter(terms, "tensor", scatter_dimension=0, tiled=True)


def local(queries, keys, values, out_weight, slot_nodes, ancestors, depth):
    parts = lax.axis_size("tensor")
    devices = lax.axis_size("node")
    features = out_weight.shape[0]
    kv_count = keys.shape[1] // HEAD
    relayed, after = None, []
    exported, table = prepare(slot_nodes, ancestors, depth, keys, values)
    got = lax.all_gather(exported, "node", axis=0, tiled=True)
    if (
        devices == 4
        and parts == 4
        and lax.axis_size("groups") == 2
        and features % (2 * HEAD) == 0
    ):
        relayed = relay(cut(out_weight), exported)
        after = relayed[:2]
    halves = []
    for kv in range(kv_count):
        halves.append(attend(kv, table, queries, keys, values, got, parts, after))
        after = halves[-1:]
    if relayed is None:
        return project_plain(halves, out_weight)
    return project_split(halves, relayed, out_weight)


def solution(mesh):
    placed = (
        P(("groups", "node"), "tensor"),
        P(("groups", "node"), "tensor"),
        P(("groups", "node"), "tensor"),
        P("node", "tensor"),
        P("groups"),
        P("groups", None),
        P("groups"),
    )
    return jax.shard_map(
        local,
        mesh=mesh,
        in_specs=placed,
        out_specs=P(("groups", "node", "tensor"), None),
        check_vma=False,
    )
```

profile of v0, /device:TPU:0, one launch (start us, length us, event | category | flops | bytes accessed | tf_op | source)
XLA Modules:
  0.0 175.2 jit_solution(2195309321818363492)
XLA Ops:
  6.6 2.8 %constant_dynamic-slice_fusion = bf16[640,1280]{1,0:T(8,128)(2,1)} fusion(bf16[1280,1280]{1,0:T(8,128)(2,1)} %refs_2_.3, s32[]{:T(128)S(6)} %select_n.3), kind=kLoop, calls=%fused_computation | loop fusion | bytes 3276804 | tf_op jit(solution)/shard_map/dynamic_slice | solution.py:440
  9.3 3.0 %collective-permute-start = (bf16[640,1280]{1,0:T(8,128)(2,1)}, bf16[640,1280]{1,0:T(8,128)(2,1)S(1)}, u32[]{:S(2)}, u32[]{:S(2)}) collective-permute-start(bf16[640,1280]{1,0:T(8,128)(2,1)} %constant_dynamic-slice_fusion), channel_id=1, source_target_pairs={{0,4},{4,0},{8,12},{12,8},{1,5},{5,1},{9,13},{13,9},{2,6},{6,2},{1... | collective-permute-start | bytes 4915208 | tf_op jit(solution)/shard_map/ppermute | solution.py:408
  13.2 1.6 prepare.1
  15.3 49.9 %collective-permute-done.refs_0_.refs_2_ = bf16[640,1280]{1,0:T(8,128)(2,1)S(1)} collective-permute-done((bf16[640,1280]{1,0:T(8,128)(2,1)}, bf16[640,1280]{1,0:T(8,128)(2,1)S(1)}, u32[]{:S(2)}, u32[]{:S(2)}) %collective-permute-start) | collective-permute-done | bytes 1638432 | tf_op jit(solution)/shard_map/ppermute | solution.py:408
  65.2 2.2 %collective-permute-start.2 = (bf16[640,1280]{1,0:T(8,128)(2,1)S(1)}, bf16[640,1280]{1,0:T(8,128)(2,1)}, u32[]{:S(2)}, u32[]{:S(2)}) collective-permute-start(bf16[640,1280]{1,0:T(8,128)(2,1)S(1)} %collective-permute-done.refs_0_.refs_2_), channel_id=1, source_target_pairs={{4,8},{8,4},{5,9},{9,5},{6,10},{10,6},{7,11},{11,7},{20,24},{24,20... | collective-permute-start | bytes 4915208 | tf_op jit(solution)/shard_map/ppermute | solution.py:412
  68.7 9.6 %attend.2.refs_0_ = bf16[4,192,640]{2,1,0:T(8,128)(2,1)} custom-call(s32[8]{0:T(128)} %copy-done.9, bf16[768,1280]{1,0:T(8,128)(2,1)} %query_hbm.3, bf16[768,256]{1,0:T(8,128)(2,1)} %keys_hbm.3, bf16[768,256]{1,0:T(8,128)(2,1)} %values_hbm.3, bf16[16,128,256]{2,1,0:T(8,128)(2,1)} %all-gather.2.cloned.1.call-done.got, bf16[640,1280]{1,0:T(8,128)(2,1)} %copy-done.2, ...), custom_call_target="tpu_custom_call" | custom-call | flops 1 | bytes 1 | tf_op jit(solution)/shard_map/attend/pallas_call | solution.py:224
  78.4 1.7 collective-permute-start.6
  80.1 9.6 %attend.3 = bf16[4,192,640]{2,1,0:T(8,128)(2,1)} custom-call(s32[8]{0:T(128)} %copy-done.9, bf16[768,1280]{1,0:T(8,128)(2,1)} %query_hbm.3, bf16[768,256]{1,0:T(8,128)(2,1)} %keys_hbm.3, bf16[768,256]{1,0:T(8,128)(2,1)} %values_hbm.3, bf16[16,128,256]{2,1,0:T(8,128)(2,1)} %all-gather.2.cloned.1.call-done.got, bf16[4,192,640]{2,1,0:T(8,128)(2,1)} %attend.2.refs_0_), custom_call_target="tpu_custom_call" | custom-call | flops 1 | bytes 1 | tf_op jit(solution)/shard_map/attend/pallas_call | solution.py:224
  89.7 4.7 %step.15 = (bf16[384,640]{1,0:T(8,128)(2,1)S(1)}, bf16[384,640]{1,0:T(8,128)(2,1)S(1)}, bf16[384,640]{1,0:T(8,128)(2,1)S(1)}, bf16[384,640]{1,0:T(8,128)(2,1)S(1...) custom-call(bf16[768,640]{1,0:T(8,128)(2,1)S(1)} %bitcast.4, bf16[768,640]{1,0:T(8,128)(2,1)} %bitcast.2.refs_1_, ...), custom_call_target="tpu_custom_call" | custom-call | flops 1 | bytes 1 | tf_op jit(solution)/shard_map/step/pallas_call | solution.py:391
  94.5 1.9 %collective-permute-done.4.refs_1_.refs_5_ = bf16[384,640]{1,0:T(8,128)(2,1)S(1)} collective-permute-done((bf16[384,640]{1,0:T(8,128)(2,1)S(1)}, bf16[384,640]{1,0:T(8,128)(2,1)S(1)}, u32[]{:S(2)}, u32[]{:S(2)}) %collective-permute-start.4) | collective-permute-done | bytes 491552 | tf_op jit(solution)/shard_map/ppermute | solution.py:248
  96.4 1.6 collective-permute-start.5
  100.1 2.5 %collective-permute-done.6.refs_4_.refs_0_ = bf16[768,640]{1,0:T(8,128)(2,1)} collective-permute-done((bf16[768,640]{1,0:T(8,128)(2,1)}, bf16[768,640]{1,0:T(8,128)(2,1)}, u32[]{:S(2)}, u32[]{:S(2)}) %collective-permute-start.6) | collective-permute-done | bytes 983072 | tf_op jit(solution)/shard_map/ppermute | solution.py:248
  102.6 1.7 step.17
  104.9 4.6 %collective-permute-done.3.refs_3_.refs_4_ = bf16[640,1280]{1,0:T(8,128)(2,1)} collective-permute-done((bf16[640,1280]{1,0:T(8,128)(2,1)S(1)}, bf16[640,1280]{1,0:T(8,128)(2,1)}, u32[]{:S(2)}, u32[]{:S(2)}) %collective-permute-start.3) | collective-permute-done | bytes 1638432 | tf_op jit(solution)/shard_map/ppermute | solution.py:411
  109.5 3.2 %step.18 = (bf16[384,640]{1,0:T(8,128)(2,1)S(1)}, bf16[384,640]{1,0:T(8,128)(2,1)S(1)}, bf16[192,640]{1,0:T(8,128)(2,1)S(1)}) custom-call(bf16[768,640]{1,0:T(8,128)(2,1)S(1)} %get-tuple-element.40.refs_0_, bf16[768,640]{1,0:T(8,128)(2,1)S(1)} %get-tuple-element.41.refs_1_, bf16[640,1280]{1,0:T(8,128)(2,1)} %collective-permute-done.2.refs_2_.refs_3_, ...), custom_call_target="tpu_custom_call" | custom-call | flops 1 | bytes 1 | tf_op jit(solution)/shard_map/step/pallas_call | solution.py:391
  112.8 1.8 %collective-permute-done.10.refs_5_.refs_7_ = bf16[384,640]{1,0:T(8,128)(2,1)S(1)} collective-permute-done((bf16[384,640]{1,0:T(8,128)(2,1)S(1)}, bf16[384,640]{1,0:T(8,128)(2,1)S(1)}, u32[]{:S(2)}, u32[]{:S(2)}) %collective-permute-start.10) | collective-permute-done | bytes 491552 | tf_op jit(solution)/shard_map/ppermute | solution.py:248
  114.8 1.6 collective-permute-start.12
  116.3 6.3 %collective-permute-done.7.refs_1_ = bf16[768,640]{1,0:T(8,128)(2,1)S(1)} collective-permute-done((bf16[768,640]{1,0:T(8,128)(2,1)}, bf16[768,640]{1,0:T(8,128)(2,1)S(1)}, u32[]{:S(2)}, u32[]{:S(2)}) %collective-permute-start.7) | collective-permute-done | bytes 983072 | tf_op jit(solution)/shard_map/ppermute | solution.py:248
  122.7 4.8 %step.20 = (bf16[384,640]{1,0:T(8,128)(2,1)S(1)}, bf16[384,640]{1,0:T(8,128)(2,1)S(1)}, bf16[384,640]{1,0:T(8,128)(2,1)S(1)}, bf16[384,640]{1,0:T(8,128)(2,1)S(1...) custom-call(bf16[768,640]{1,0:T(8,128)(2,1)} %collective-permute-done.6.refs_4_.refs_0_, ...), custom_call_target="tpu_custom_call" | custom-call | flops 1 | bytes 1 | tf_op jit(solution)/shard_map/step/pallas_call | solution.py:391
  129.4 4.0 %collective-permute-done.12.refs_8_ = bf16[192,1920]{1,0:T(8,128)(2,1)S(1)} collective-permute-done((bf16[192,1920]{1,0:T(8,128)(2,1)S(1)}, bf16[192,1920]{1,0:T(8,128)(2,1)S(1)}, u32[]{:S(2)}, u32[]{:S(2)}) %collective-permute-start.12) | collective-permute-done | bytes 737312 | tf_op jit(solution)/shard_map/ppermute | solution.py:248
  133.7 1.6 collective-permute-start.14
  135.3 5.7 %collective-permute-done.14.refs_4_ = bf16[192,640]{1,0:T(8,128)(2,1)S(1)} collective-permute-done((bf16[192,640]{1,0:T(8,128)(2,1)S(1)}, bf16[192,640]{1,0:T(8,128)(2,1)S(1)}, u32[]{:S(2)}, u32[]{:S(2)}) %collective-permute-start.14) | collective-permute-done | bytes 245792 | tf_op jit(solution)/shard_map/ppermute | solution.py:248
  141.1 1.6 collective-permute-start.15
  142.7 1.5 collective-permute-start.16
  144.3 1.7 step.23
  147.4 1.5 collective-permute-done.16.refs_2_
  149.0 1.7 step.25
  151.4 1.6 collective-permute-start.20
  154.3 4.9 %collective-permute-done.18.refs_4_.refs_5_ = bf16[192,640]{1,0:T(8,128)(2,1)S(1)} collective-permute-done((bf16[192,640]{1,0:T(8,128)(2,1)S(1)}, bf16[192,640]{1,0:T(8,128)(2,1)S(1)}, u32[]{:S(2)}, u32[]{:S(2)}) %collective-permute-start.18) | collective-permute-done | bytes 245792 | tf_op jit(solution)/shard_map/ppermute | solution.py:248
  160.4 1.6 collective-permute-start.22
  162.0 2.8 %collective-permute-done.23.refs_2_ = bf16[192,640]{1,0:T(8,128)(2,1)S(1)} collective-permute-done((bf16[192,640]{1,0:T(8,128)(2,1)S(1)}, bf16[192,640]{1,0:T(8,128)(2,1)S(1)}, u32[]{:S(2)}, u32[]{:S(2)}) %collective-permute-start.23) | collective-permute-done | bytes 245792 | tf_op jit(solution)/shard_map/ppermute | solution.py:248
  164.9 2.0 %collective-permute-done.22.refs_6_ = bf16[192,640]{1,0:T(8,128)(2,1)S(1)} collective-permute-done((bf16[192,640]{1,0:T(8,128)(2,1)S(1)}, bf16[192,640]{1,0:T(8,128)(2,1)S(1)}, u32[]{:S(2)}, u32[]{:S(2)}) %collective-permute-start.22) | collective-permute-done | bytes 245792 | tf_op jit(solution)/shard_map/ppermute | solution.py:248
  (63 shorter events, 14.5 us)
Async XLA Ops:
  6.5 62.2 %all-gather.2.cloned.1.call-start = ((), (), s32[]{:S(2)}) async-start(), calls=%async_computation | async-start | bytes 1310720 | tf_op jit(solution)/shard_map/all_gather | solution.py:534
  6.5 6.6 %copy-start.8 = (s32[24,7]{0,1:T(8,128)S(1)}, s32[24,7]{0,1:T(8,128)}, u32[]{:S(2)}) copy-start(s32[24,7]{0,1:T(8,128)} %param.12) | copy-start | bytes 2020
  6.5 6.6 %copy-start.10 = (s32[24]{0:T(128)S(1)}, s32[24]{0:T(128)}, u32[]{:S(2)}) copy-start(s32[24]{0:T(128)} %refs_0_.1) | copy-start | bytes 292
  6.5 6.6 %copy-start.11 = (s32[24]{0:T(128)S(1)}, s32[24]{0:T(128)}, u32[]{:S(2)}) copy-start(s32[24]{0:T(128)} %refs_2_.2) | copy-start | bytes 292
  9.3 55.9 %collective-permute-start = (bf16[640,1280]{1,0:T(8,128)(2,1)}, bf16[640,1280]{1,0:T(8,128)(2,1)S(1)}, u32[]{:S(2)}, u32[]{:S(2)}) collective-permute-start(bf16[640,1280]{1,0:T(8,128)(2,1)} %constant_dynamic-slice_fusion), channel_id=1, source_target_pairs={{0,4},{4,0},{8,12},{12,8},{1,5},{5,1},{9,13},{13,9},{2,6},{6,2},{1... | collective-permute-start | bytes 4915208 | tf_op jit(solution)/shard_map/ppermute | solution.py:408
  12.4 52.9 %collective-permute-start.1 = (bf16[640,1280]{1,0:T(8,128)(2,1)}, bf16[640,1280]{1,0:T(8,128)(2,1)S(1)}, u32[]{:S(2)}, u32[]{:S(2)}) collective-permute-start(bf16[640,1280]{1,0:T(8,128)(2,1)} %constant_dynamic-slice_fusion), channel_id=1, source_target_pairs={{4,8},{8,4},{5,9},{9,5},{6,10},{10,6},{7,11},{11,7},{20,24},{24,20... | collective-permute-start | bytes 4915208 | tf_op jit(solution)/shard_map/ppermute | solution.py:409
  65.2 33.4 %collective-permute-start.2 = (bf16[640,1280]{1,0:T(8,128)(2,1)S(1)}, bf16[640,1280]{1,0:T(8,128)(2,1)}, u32[]{:S(2)}, u32[]{:S(2)}) collective-permute-start(bf16[640,1280]{1,0:T(8,128)(2,1)S(1)} %collective-permute-done.refs_0_.refs_2_), channel_id=1, source_target_pairs={{4,8},{8,4},{5,9},{9,5},{6,10},{10,6},{7,11},{11,7},{20,24},{24,20... | collective-permute-start | bytes 4915208 | tf_op jit(solution)/shard_map/ppermute | solution.py:412
  67.4 42.1 %collective-permute-start.3 = (bf16[640,1280]{1,0:T(8,128)(2,1)S(1)}, bf16[640,1280]{1,0:T(8,128)(2,1)}, u32[]{:S(2)}, u32[]{:S(2)}) collective-permute-start(bf16[640,1280]{1,0:T(8,128)(2,1)S(1)} %collective-permute-done.1.refs_1_.refs_2_), channel_id=1, source_target_pairs={{4,0},{8,12},{5,1},{9,13},{6,2},{10,14},{7,3},{11,15},{20,16},{24,... | collective-permute-start | bytes 4915208 | tf_op jit(solution)/shard_map/ppermute | solution.py:411
  78.3 11.4 %copy-start.4 = (bf16[4,192,640]{2,1,0:T(8,128)(2,1)S(1)}, bf16[4,192,640]{2,1,0:T(8,128)(2,1)}, u32[]{:S(2)}) copy-start(bf16[4,192,640]{2,1,0:T(8,128)(2,1)} %attend.2.refs_0_) | copy-start | bytes 2949124
  78.4 11.4 %copy-start.5 = (bf16[1280,1280]{1,0:T(8,128)(2,1)S(1)}, bf16[1280,1280]{1,0:T(8,128)(2,1)}, u32[]{:S(2)}) copy-start(bf16[1280,1280]{1,0:T(8,128)(2,1)} %refs_2_.3) | copy-start | bytes 9830404
  78.4 24.2 %collective-permute-start.6 = (bf16[768,640]{1,0:T(8,128)(2,1)}, bf16[768,640]{1,0:T(8,128)(2,1)}, u32[]{:S(2)}, u32[]{:S(2)}) collective-permute-start(bf16[768,640]{1,0:T(8,128)(2,1)} %bitcast.3), channel_id=1, source_target_pairs={{0,16},{16,0},{1,17},{17,1},{2,18},{18,2},{3,19},{19,3},{4,20},{20... | collective-permute-start | bytes 2949128 | tf_op jit(solution)/shard_map/ppermute | solution.py:248
  89.7 12.8 %copy-start.3 = (bf16[640,1280]{1,0:T(8,128)(2,1)S(1)}, bf16[640,1280]{1,0:T(8,128)(2,1)}, u32[]{:S(2)}) copy-start(bf16[640,1280]{1,0:T(8,128)(2,1)} %copy-done.2) | copy-start | bytes 4915204
  94.5 1.9 %collective-permute-start.4 = (bf16[384,640]{1,0:T(8,128)(2,1)S(1)}, bf16[384,640]{1,0:T(8,128)(2,1)S(1)}, u32[]{:S(2)}, u32[]{:S(2)}) collective-permute-start(bf16[384,640]{1,0:T(8,128)(2,1)S(1)} %get-tuple-element.43), channel_id=1, source_target_pairs={{0,1},{1,0},{2,3},{3,2},{4,5},{5,4},{6,7},{7,6},{8,9},{9,8},{10,11... | collective-permute-start | bytes 1474568 | tf_op jit(solution)/shard_map/ppermute | solution.py:248
  96.4 8.1 %collective-permute-start.5 = (bf16[192,640]{1,0:T(8,128)(2,1)S(1)}, bf16[192,640]{1,0:T(8,128)(2,1)S(1)}, u32[]{:S(2)}, u32[]{:S(2)}) collective-permute-start(bf16[192,640]{1,0:T(8,128)(2,1)S(1)} %step.16.refs_3_), channel_id=1, source_target_pairs={{0,2},{1,3},{2,0},{3,1},{4,6},{5,7},{6,4},{7,5},{8,10},{9,11},{10,... | collective-permute-start | bytes 737288 | tf_op jit(solution)/shard_map/ppermute | solution.py:248
  98.0 24.7 %collective-permute-start.7 = (bf16[768,640]{1,0:T(8,128)(2,1)}, bf16[768,640]{1,0:T(8,128)(2,1)S(1)}, u32[]{:S(2)}, u32[]{:S(2)}) collective-permute-start(bf16[768,640]{1,0:T(8,128)(2,1)} %bitcast.2.refs_1_), channel_id=1, source_target_pairs={{0,16},{16,0},{1,17},{17,1},{2,18},{18,2},{3,19},{19,3},{4,20},{20... | collective-permute-start | bytes 2949128 | tf_op jit(solution)/shard_map/ppermute | solution.py:248
  98.6 45.7 %collective-permute-start.17 = (bf16[640,1280]{1,0:T(8,128)(2,1)}, bf16[640,1280]{1,0:T(8,128)(2,1)S(1)}, u32[]{:S(2)}, u32[]{:S(2)}) collective-permute-start(bf16[640,1280]{1,0:T(8,128)(2,1)} %collective-permute-done.2.refs_2_.refs_3_), channel_id=1, source_target_pairs={{4,0},{8,12},{5,1},{9,13},{6,2},{10,14},{7,3},{11,15},{20,16},{24,... | collective-permute-start | bytes 4915208 | tf_op jit(solution)/shard_map/ppermute | solution.py:449
  102.5 10.2 %collective-permute-start.8 = (bf16[384,640]{1,0:T(8,128)(2,1)S(1)}, bf16[384,640]{1,0:T(8,128)(2,1)S(1)}, u32[]{:S(2)}, u32[]{:S(2)}) collective-permute-start(bf16[384,640]{1,0:T(8,128)(2,1)S(1)} %get-tuple-element.47), channel_id=1, source_target_pairs={{0,1},{1,0},{2,3},{3,2},{4,5},{5,4},{6,7},{7,6},{8,9},{9,8},{10,11... | collective-permute-start | bytes 1474568 | tf_op jit(solution)/shard_map/ppermute | solution.py:248
  104.5 8.2 %collective-permute-start.9 = (bf16[384,640]{1,0:T(8,128)(2,1)S(1)}, bf16[384,640]{1,0:T(8,128)(2,1)S(1)}, u32[]{:S(2)}, u32[]{:S(2)}) collective-permute-start(bf16[384,640]{1,0:T(8,128)(2,1)S(1)} %get-tuple-element.44.refs_7_), channel_id=1, source_target_pairs={{0,1},{1,0},{2,3},{3,2},{4,5},{5,4},{6,7},{7,6},{8,9},{9,8},{10,11... | collective-permute-start | bytes 1474568 | tf_op jit(solution)/shard_map/ppermute | solution.py:248
  112.7 1.9 %collective-permute-start.10 = (bf16[384,640]{1,0:T(8,128)(2,1)S(1)}, bf16[384,640]{1,0:T(8,128)(2,1)S(1)}, u32[]{:S(2)}, u32[]{:S(2)}) collective-permute-start(bf16[384,640]{1,0:T(8,128)(2,1)S(1)} %get-tuple-element.50), channel_id=1, source_target_pairs={{0,1},{1,0},{2,3},{3,2},{4,5},{5,4},{6,7},{7,6},{8,9},{9,8},{10,11... | collective-permute-start | bytes 1474568 | tf_op jit(solution)/shard_map/ppermute | solution.py:248
  114.8 18.6 %collective-permute-start.12 = (bf16[192,1920]{1,0:T(8,128)(2,1)S(1)}, bf16[192,1920]{1,0:T(8,128)(2,1)S(1)}, u32[]{:S(2)}, u32[]{:S(2)}) collective-permute-start(bf16[192,1920]{1,0:T(8,128)(2,1)S(1)} %step.19.refs_5_), channel_id=1, source_target_pairs={{0,2},{1,3},{2,0},{3,1},{4,6},{5,7},{6,4},{7,5},{8,10},{9,11},{10,... | collective-permute-start | bytes 2211848 | tf_op jit(solution)/shard_map/ppermute | solution.py:248
  127.5 1.9 %collective-permute-start.11 = (bf16[384,640]{1,0:T(8,128)(2,1)S(1)}, bf16[384,640]{1,0:T(8,128)(2,1)S(1)}, u32[]{:S(2)}, u32[]{:S(2)}) collective-permute-start(bf16[384,640]{1,0:T(8,128)(2,1)S(1)} %get-tuple-element.52), channel_id=1, source_target_pairs={{0,1},{1,0},{2,3},{3,2},{4,5},{5,4},{6,7},{7,6},{8,9},{9,8},{10,11... | collective-permute-start | bytes 1474568 | tf_op jit(solution)/shard_map/ppermute | solution.py:248
  127.5 7.7 %collective-permute-start.13 = (bf16[384,640]{1,0:T(8,128)(2,1)S(1)}, bf16[384,640]{1,0:T(8,128)(2,1)S(1)}, u32[]{:S(2)}, u32[]{:S(2)}) collective-permute-start(bf16[384,640]{1,0:T(8,128)(2,1)S(1)} %get-tuple-element.57), channel_id=1, source_target_pairs={{0,1},{1,0},{2,3},{3,2},{4,5},{5,4},{6,7},{7,6},{8,9},{9,8},{10,11... | collective-permute-start | bytes 1474568 | tf_op jit(solution)/shard_map/ppermute | solution.py:248
  133.7 10.6 %copy-start.1 = (bf16[640,1280]{1,0:T(8,128)(2,1)S(1)}, bf16[640,1280]{1,0:T(8,128)(2,1)}, u32[]{:S(2)}) copy-start(bf16[640,1280]{1,0:T(8,128)(2,1)} %copy-done) | copy-start | bytes 4915204
  133.7 7.2 %collective-permute-start.14 = (bf16[192,640]{1,0:T(8,128)(2,1)S(1)}, bf16[192,640]{1,0:T(8,128)(2,1)S(1)}, u32[]{:S(2)}, u32[]{:S(2)}) collective-permute-start(bf16[192,640]{1,0:T(8,128)(2,1)S(1)} %get-tuple-element.58), channel_id=1, source_target_pairs={{0,2},{1,3},{2,0},{3,1},{4,6},{5,7},{6,4},{7,5},{8,10},{9,11},{10,... | collective-permute-start | bytes 737288 | tf_op jit(solution)/shard_map/ppermute | solution.py:248
  141.1 6.3 %collective-permute-start.15 = (bf16[192,640]{1,0:T(8,128)(2,1)S(1)}, bf16[192,640]{1,0:T(8,128)(2,1)S(1)}, u32[]{:S(2)}, u32[]{:S(2)}) collective-permute-start(bf16[192,640]{1,0:T(8,128)(2,1)S(1)} %get-tuple-element.59), channel_id=1, source_target_pairs={{0,16},{16,0},{1,17},{17,1},{2,18},{18,2},{3,19},{19,3},{4,20},{20... | collective-permute-start | bytes 737288 | tf_op jit(solution)/shard_map/ppermute | solution.py:248
  142.7 6.2 %collective-permute-start.16 = (bf16[192,640]{1,0:T(8,128)(2,1)S(1)}, bf16[192,640]{1,0:T(8,128)(2,1)S(1)}, u32[]{:S(2)}, u32[]{:S(2)}) collective-permute-start(bf16[192,640]{1,0:T(8,128)(2,1)S(1)} %get-tuple-element.60.refs_4_), channel_id=1, source_target_pairs={{0,2},{1,3},{2,0},{3,1},{4,6},{5,7},{6,4},{7,5},{8,10},{9,11},{10,... | collective-permute-start | bytes 737288 | tf_op jit(solution)/shard_map/ppermute | solution.py:248
  146.1 5.3 %collective-permute-start.19 = (bf16[384,640]{1,0:T(8,128)(2,1)S(1)}, bf16[384,640]{1,0:T(8,128)(2,1)S(1)}, u32[]{:S(2)}, u32[]{:S(2)}) collective-permute-start(bf16[384,640]{1,0:T(8,128)(2,1)S(1)} %get-tuple-element.63.refs_3_), channel_id=1, source_target_pairs={{0,1},{1,0},{2,3},{3,2},{4,5},{5,4},{6,7},{7,6},{8,9},{9,8},{10,11... | collective-permute-start | bytes 1474568 | tf_op jit(solution)/shard_map/ppermute | solution.py:248
  150.7 2.3 %collective-permute-start.21 = (bf16[384,640]{1,0:T(8,128)(2,1)S(1)}, bf16[384,640]{1,0:T(8,128)(2,1)S(1)}, u32[]{:S(2)}, u32[]{:S(2)}) collective-permute-start(bf16[384,640]{1,0:T(8,128)(2,1)S(1)} %get-tuple-element.65.refs_2_), channel_id=1, source_target_pairs={{0,1},{1,0},{2,3},{3,2},{4,5},{5,4},{6,7},{7,6},{8,9},{9,8},{10,11... | collective-permute-start | bytes 1474568 | tf_op jit(solution)/shard_map/ppermute | solution.py:248
  150.8 8.4 %collective-permute-start.18 = (bf16[192,640]{1,0:T(8,128)(2,1)S(1)}, bf16[192,640]{1,0:T(8,128)(2,1)S(1)}, u32[]{:S(2)}, u32[]{:S(2)}) collective-permute-start(bf16[192,640]{1,0:T(8,128)(2,1)S(1)} %step.24.refs_4_), channel_id=1, source_target_pairs={{0,16},{16,0},{1,17},{17,1},{2,18},{18,2},{3,19},{19,3},{4,20},{20... | collective-permute-start | bytes 737288 | tf_op jit(solution)/shard_map/ppermute | solution.py:248
  151.4 8.9 %collective-permute-start.20 = (bf16[192,640]{1,0:T(8,128)(2,1)S(1)}, bf16[192,640]{1,0:T(8,128)(2,1)S(1)}, u32[]{:S(2)}, u32[]{:S(2)}) collective-permute-start(bf16[192,640]{1,0:T(8,128)(2,1)S(1)} %step.26.refs_2_), channel_id=1, source_target_pairs={{0,2},{1,3},{2,0},{3,1},{4,6},{5,7},{6,4},{7,5},{8,10},{9,11},{10,... | collective-permute-start | bytes 737288 | tf_op jit(solution)/shard_map/ppermute | solution.py:248
  153.1 11.7 %collective-permute-start.23 = (bf16[192,640]{1,0:T(8,128)(2,1)S(1)}, bf16[192,640]{1,0:T(8,128)(2,1)S(1)}, u32[]{:S(2)}, u32[]{:S(2)}) collective-permute-start(bf16[192,640]{1,0:T(8,128)(2,1)S(1)} %step.27.refs_3_), channel_id=1, source_target_pairs={{0,2},{1,3},{2,0},{3,1},{4,6},{5,7},{6,4},{7,5},{8,10},{9,11},{10,... | collective-permute-start | bytes 737288 | tf_op jit(solution)/shard_map/ppermute | solution.py:248
  160.4 6.5 %collective-permute-start.22 = (bf16[192,640]{1,0:T(8,128)(2,1)S(1)}, bf16[192,640]{1,0:T(8,128)(2,1)S(1)}, u32[]{:S(2)}, u32[]{:S(2)}) collective-permute-start(bf16[192,640]{1,0:T(8,128)(2,1)S(1)} %step.28.refs_3_), channel_id=1, source_target_pairs={{0,16},{16,0},{1,17},{17,1},{2,18},{18,2},{3,19},{19,3},{4,20},{20... | collective-permute-start | bytes 737288 | tf_op jit(solution)/shard_map/ppermute | solution.py:248
  (5 other events, 20.8 us)
Sparse Core Ops, SparseCore 0:
  15.5 43.9 all-gather.1
where the time goes:
time: 176 us; the launch traced here: 175 us
  waiting for transfers between devices  92 us (52%)
  Pallas kernels  41.2 us (23%)
  starting transfers between devices  24.9 us (14%)
  between operations  13.7 us (8%)
  local copies, waits for them, and re-layouts  3.4 us (2%)
    ppermute x1, waiting for transfers between devices, relay(): near = lax.ppermute(piece, 'node', PAIRS)  49.9 us
    ppermute x19, waiting for transfers between devices, swap(): return lax.ppermute(array, axis, [(i, i ^ distance) for i in range(size)])  37.3 us
    pallas_call x2, Pallas kernels, attend(): pl.pallas_call(functools.partial(attend_body, kv, parts), out_shape=jax.S...  19.2 us
    pallas_call x15, Pallas kernels, step(): pl.pallas_call(functools.partial(step_body, plan), out_shape=[jax.ShapeDt...  18.9 us
    ppermute x19, starting transfers between devices, swap(): return lax.ppermute(array, axis, [(i, i ^ distance) for i in range(size)])  16.2 us
    ppermute x1, waiting for transfers between devices, relay(): across_out = lax.ppermute(across, 'node', OUTWARD)  4.63 us
  transfers between devices with their start and end apart: 25, of which 17 were waited for; matrix products, arithmetic and copies ran while one was open for 0% of the time, Pallas kernels for 23%

commit v1 on v0

--- a/solution.py
+++ b/solution.py
@@ -17,7 +17,7 @@
 DEAD = -1e30
 LIGHT = pl.CostEstimate(flops=1, bytes_accessed=1, transcendentals=0)
 VMEM_LIMIT = 20 * 1024 * 1024
-ATTEND_LIMIT = 56 * 1024 * 1024
+ATTEND_LIMIT = 24 * 1024 * 1024
 
 
 def prepare_body(nodes, *refs):
@@ -215,6 +215,10 @@
     return jnp.where(distance % 2 == 1, distance // 2, half + distance // 2)
 
 
+def in_hbm(array):
+    return pltpu.with_memory_space_constraint(array, pltpu.HBM)
+
+
 def attend(kv, table, queries, keys, values, got, parts, after):
     rows = queries.shape[0]
     width = queries.shape[1] // (keys.shape[1] // HEAD)
@@ -240,7 +244,7 @@
         compiler_params=pltpu.CompilerParams(vmem_limit_bytes=ATTEND_LIMIT),
         cost_estimate=LIGHT,
         name="attend",
-    )(table, queries, keys, values, got, *after)
+    )(table, *[in_hbm(x) for x in (queries, keys, values, got)], *after)
 
 
 def swap(array, axis, distance):
@@ -308,10 +312,6 @@
                     pl.when(pick)(pltpu.make_async_copy(source, target, sem).start)
                     column += count
     made = [[(outs.pop(0), outs.pop(0)) for _ in rows] for _ in weights]
-    if plan["hold"]:
-        for part in [x for parts in rows for x in parts]:
-            out = outs.pop(0)
-            out[...] = part[...]
     for bundle in cores:
         out, column = outs.pop(0), 0
         for pair in bundle:
@@ -338,7 +338,7 @@
                 product(parts, weight[0], sent, kept)
 
 
-def step(rows=(), weights=(), cores=(), chips=(), after=(), hold=False, direct=False):
+def step(rows=(), weights=(), cores=(), chips=(), after=(), direct=False):
     weights = [weight if isinstance(weight, tuple) else (weight,) for weight in weights]
     arrays, fetch, plans = [], [], []
     for weight in weights:
@@ -356,8 +356,6 @@
     shapes = []
     for width in widths:
         shapes += [(parts[0].shape[0] // 2, width) for parts in rows for _ in range(2)]
-    if hold:
-        shapes += [part.shape for parts in rows for part in parts]
     for bundle in cores:
         shapes.append((bundle[0][0].shape[0] // 2, sum(kept.shape[1] for kept, _ in bundle)))
     for bundle in chips:
@@ -370,7 +368,6 @@
         "chips": [len(bundle) - 1 for bundle in chips],
         "after": len(after),
         "outs": len(shapes),
-        "hold": hold,
         "direct": direct,
     }
     vmem, hbm = pl.BlockSpec(memory_space=pltpu.VMEM), pl.BlockSpec(memory_space=pl.ANY)
@@ -463,8 +460,8 @@
     second = (whole(near_across), whole(across_out))
     far = (whole(across), whole(far_out))
 
-    sent_a, kept_a, sent_b, kept_b, *rows = step(
-        [rows], [[(out_weight, 0, half)], [(out_weight, half, half)]], hold=True
+    sent_a, kept_a, sent_b, kept_b = step(
+        [rows], [[(out_weight, 0, half)], [(out_weight, half, half)]]
     )
     one = [(kept_a, core(sent_a))]
     (away,) = step(cores=[one])
@@ -474,9 +471,7 @@
     two = [(kept_b, core(sent_b)), (kept_1, core(sent_1)), (kept_2, core(sent_2))]
     (away,) = step(cores=[two])
     two.append(chip(away))
-    sent_3, kept_3, sent_4, kept_4, *other = step(
-        [other], [whole(near), second], after=[away], hold=True
-    )
+    sent_3, kept_3, sent_4, kept_4 = step([other], [whole(near), second], after=[away])
     three, four = [(kept_3, core(sent_3))], [(kept_4, core(sent_4))]
     away, done_b, done_1, done_2 = step(cores=[three], chips=[two])
     three.append(chip(away))

time: 176 us -> 176 us (level)
  waiting for transfers between devices: 92 us -> 97 us
  Pallas kernels: 41.2 us -> 36.9 us
    ppermute x19, waiting for transfers between devices: 37.3 us -> 40.6 us  [swap(): return lax.ppermute(array, axis, [(i, i ^ distance) for i in range(size)])]
    pallas_call x2, Pallas kernels: 19.2 us -> 16.7 us  [attend(): pl.pallas_call(functools.partial(attend_body, kv, parts), out_shape=jax.S...]
  transfers between devices with their start and end apart: 25 -> 25, of which waited for: 17 -> 16; matrix products, arithmetic and copies ran while one was open for 0% -> 0% of each run, Pallas kernels for 23% -> 20%
where the time goes in v1:
time: 176 us; the launch traced here: 175 us
  waiting for transfers between devices  97 us (55%)
  Pallas kernels  36.9 us (21%)
  starting transfers between devices  24.8 us (14%)
  between operations  13.7 us (8%)
  local copies, waits for them, and re-layouts  2.8 us (2%)
    ppermute x1, waiting for transfers between devices, relay(): near = lax.ppermute(piece, 'node', PAIRS)  50.5 us
    ppermute x19, waiting for transfers between devices, swap(): return lax.ppermute(array, axis, [(i, i ^ distance) for i in range(size)])  40.6 us
    pallas_call x15, Pallas kernels, step(): pl.pallas_call(functools.partial(step_body, plan), out_shape=[jax.ShapeDt...  17.2 us
    pallas_call x2, Pallas kernels, attend(): pl.pallas_call(functools.partial(attend_body, kv, parts), out_shape=jax.S...  16.7 us
    ppermute x19, starting transfers between devices, swap(): return lax.ppermute(array, axis, [(i, i ^ distance) for i in range(size)])  16.4 us
    ppermute x1, waiting for transfers between devices, relay(): across_out = lax.ppermute(across, 'node', OUTWARD)  5.68 us
  transfers between devices with their start and end apart: 25, of which 16 were waited for; matrix products, arithmetic and copies ran while one was open for 0% of the time, Pallas kernels for 20%

profile of v1, /device:TPU:0, one launch (start us, length us, event | category | flops | bytes accessed | tf_op | source)
XLA Modules:
  0.0 175.1 jit_solution(6055176905605054538)
XLA Ops:
  6.6 2.8 %constant_dynamic-slice_fusion = bf16[640,1280]{1,0:T(8,128)(2,1)} fusion(bf16[1280,1280]{1,0:T(8,128)(2,1)} %refs_2_.3, s32[]{:T(128)S(6)} %select_n.3), kind=kLoop, calls=%fused_computation | loop fusion | bytes 3276804 | tf_op jit(solution)/shard_map/dynamic_slice | solution.py:437
  9.3 3.0 %collective-permute-start = (bf16[640,1280]{1,0:T(8,128)(2,1)}, bf16[640,1280]{1,0:T(8,128)(2,1)S(1)}, u32[]{:S(2)}, u32[]{:S(2)}) collective-permute-start(bf16[640,1280]{1,0:T(8,128)(2,1)} %constant_dynamic-slice_fusion), channel_id=1, source_target_pairs={{0,4},{4,0},{8,12},{12,8},{1,5},{5,1},{9,13},{13,9},{2,6},{6,2},{1... | collective-permute-start | bytes 4915208 | tf_op jit(solution)/shard_map/ppermute | solution.py:405
  13.2 1.6 prepare.1
  14.8 50.5 %collective-permute-done.refs_0_.refs_2_ = bf16[640,1280]{1,0:T(8,128)(2,1)S(1)} collective-permute-done((bf16[640,1280]{1,0:T(8,128)(2,1)}, bf16[640,1280]{1,0:T(8,128)(2,1)S(1)}, u32[]{:S(2)}, u32[]{:S(2)}) %collective-permute-start) | collective-permute-done | bytes 1638432 | tf_op jit(solution)/shard_map/ppermute | solution.py:405
  65.2 1.8 %collective-permute-start.2 = (bf16[640,1280]{1,0:T(8,128)(2,1)S(1)}, bf16[640,1280]{1,0:T(8,128)(2,1)}, u32[]{:S(2)}, u32[]{:S(2)}) collective-permute-start(bf16[640,1280]{1,0:T(8,128)(2,1)S(1)} %collective-permute-done.refs_0_.refs_2_), channel_id=1, source_target_pairs={{4,8},{8,4},{5,9},{9,5},{6,10},{10,6},{7,11},{11,7},{20,24},{24,20... | collective-permute-start | bytes 4915208 | tf_op jit(solution)/shard_map/ppermute | solution.py:409
  68.4 8.3 %attend.2.refs_0_ = bf16[4,192,640]{2,1,0:T(8,128)(2,1)S(1)} custom-call(s32[8]{0:T(128)S(1)} %get-tuple-element.32.table, bf16[768,1280]{1,0:T(8,128)(2,1)} %query_hbm.3, bf16[768,256]{1,0:T(8,128)(2,1)} %keys_hbm.3, bf16[768,256]{1,0:T(8,128)(2,1)} %values_hbm.3, bf16[16,128,256]{2,1,0:T(8,128)(2,1)} %all-gather.2.cloned.1.call-done.got, ...), custom_call_target="tpu_custom_call" | custom-call | flops 1 | bytes 1 | tf_op jit(solution)/shard_map/attend/pallas_call | solution.py:228
  76.7 1.8 %collective-permute-start.6 = (bf16[768,640]{1,0:T(8,128)(2,1)S(1)}, bf16[768,640]{1,0:T(8,128)(2,1)S(1)}, u32[]{:S(2)}, u32[]{:S(2)}) collective-permute-start(bf16[768,640]{1,0:T(8,128)(2,1)S(1)} %bitcast.3), channel_id=1, source_target_pairs={{0,16},{16,0},{1,17},{17,1},{2,18},{18,2},{3,19},{19,3},{4,20},{20... | collective-permute-start | bytes 2949128 | tf_op jit(solution)/shard_map/ppermute | solution.py:252
  78.5 8.3 %attend.3 = bf16[4,192,640]{2,1,0:T(8,128)(2,1)S(1)} custom-call(s32[8]{0:T(128)S(1)} %get-tuple-element.32.table, bf16[768,1280]{1,0:T(8,128)(2,1)} %query_hbm.3, bf16[768,256]{1,0:T(8,128)(2,1)} %keys_hbm.3, bf16[768,256]{1,0:T(8,128)(2,1)} %values_hbm.3, bf16[16,128,256]{2,1,0:T(8,128)(2,1)} %all-gather.2.cloned.1.call-done.got, ...), custom_call_target="tpu_custom_call" | custom-call | flops 1 | bytes 1 | tf_op jit(solution)/shard_map/attend/pallas_call | solution.py:228
  86.9 3.2 %step.15 = (bf16[384,640]{1,0:T(8,128)(2,1)S(1)}, bf16[384,640]{1,0:T(8,128)(2,1)S(1)}, bf16[384,640]{1,0:T(8,128)(2,1)S(1)}, bf16[384,640]{1,0:T(8,128)(2,1)S(1)}) custom-call(bf16[768,640]{1,0:T(8,128)(2,1)S(1)} %bitcast.4, bf16[768,640]{1,0:T(8,128)(2,1)S(1)} %bitcast.8, bf16[1280,1280]{1,0:T(8,128)(2,1)S(1)} %copy-done), custom_call_target="tpu_custom_call" | custom-call | flops 1 | bytes 1 | tf_op jit(solution)/shard_map/step/pallas_call | solution.py:388
  90.2 1.9 %collective-permute-done.4.refs_1_.refs_5_ = bf16[384,640]{1,0:T(8,128)(2,1)S(1)} collective-permute-done((bf16[384,640]{1,0:T(8,128)(2,1)S(1)}, bf16[384,640]{1,0:T(8,128)(2,1)S(1)}, u32[]{:S(2)}, u32[]{:S(2)}) %collective-permute-start.4) | collective-permute-done | bytes 491552 | tf_op jit(solution)/shard_map/ppermute | solution.py:252
  92.1 1.6 collective-permute-start.5
  95.7 5.8 %collective-permute-done.6.refs_4_.refs_0_ = bf16[768,640]{1,0:T(8,128)(2,1)S(1)} collective-permute-done((bf16[768,640]{1,0:T(8,128)(2,1)S(1)}, bf16[768,640]{1,0:T(8,128)(2,1)S(1)}, u32[]{:S(2)}, u32[]{:S(2)}) %collective-permute-start.6) | collective-permute-done | bytes 983072 | tf_op jit(solution)/shard_map/ppermute | solution.py:252
  101.5 1.7 step.17
  103.8 5.7 %collective-permute-done.3.refs_3_.refs_4_ = bf16[640,1280]{1,0:T(8,128)(2,1)} collective-permute-done((bf16[640,1280]{1,0:T(8,128)(2,1)S(1)}, bf16[640,1280]{1,0:T(8,128)(2,1)}, u32[]{:S(2)}, u32[]{:S(2)}) %collective-permute-start.3) | collective-permute-done | bytes 1638432 | tf_op jit(solution)/shard_map/ppermute | solution.py:408
  109.5 3.2 %step.18 = (bf16[384,640]{1,0:T(8,128)(2,1)S(1)}, bf16[384,640]{1,0:T(8,128)(2,1)S(1)}, bf16[192,640]{1,0:T(8,128)(2,1)S(1)}) custom-call(bf16[768,640]{1,0:T(8,128)(2,1)S(1)} %bitcast.6, bf16[768,640]{1,0:T(8,128)(2,1)S(1)} %bitcast.11, bf16[640,1280]{1,0:T(8,128)(2,1)} %collective-permute-done.2.refs_2_.refs_3_, ...), custom_call_target="tpu_custom_call" | custom-call | flops 1 | bytes 1 | tf_op jit(solution)/shard_map/step/pallas_call | solution.py:388
  112.8 1.8 %collective-permute-done.10.refs_5_.refs_7_ = bf16[384,640]{1,0:T(8,128)(2,1)S(1)} collective-permute-done((bf16[384,640]{1,0:T(8,128)(2,1)S(1)}, bf16[384,640]{1,0:T(8,128)(2,1)S(1)}, u32[]{:S(2)}, u32[]{:S(2)}) %collective-permute-start.10) | collective-permute-done | bytes 491552 | tf_op jit(solution)/shard_map/ppermute | solution.py:252
  114.8 1.6 collective-permute-start.12
  116.3 4.5 %collective-permute-done.7.refs_1_ = bf16[768,640]{1,0:T(8,128)(2,1)S(1)} collective-permute-done((bf16[768,640]{1,0:T(8,128)(2,1)S(1)}, bf16[768,640]{1,0:T(8,128)(2,1)S(1)}, u32[]{:S(2)}, u32[]{:S(2)}) %collective-permute-start.7) | collective-permute-done | bytes 983072 | tf_op jit(solution)/shard_map/ppermute | solution.py:252
  120.8 4.6 %step.20 = (bf16[384,640]{1,0:T(8,128)(2,1)S(1)}, bf16[384,640]{1,0:T(8,128)(2,1)S(1)}, bf16[384,640]{1,0:T(8,128)(2,1)S(1)}, bf16[384,640]{1,0:T(8,128)(2,1)S(1)}) custom-call(bf16[768,640]{1,0:T(8,128)(2,1)S(1)} %collective-permute-done.6.refs_4_.refs_0_, bf16[768,640]{1,0:T(8,128)(2,1)S(1)} %collective-permute-done.7.refs_1_, ...), custom_call_target="tpu_custom_call" | custom-call | flops 1 | bytes 1 | tf_op jit(solution)/shard_map/step/pallas_call | solution.py:388
  127.3 6.0 %collective-permute-done.12.refs_8_ = bf16[192,1920]{1,0:T(8,128)(2,1)S(1)} collective-permute-done((bf16[192,1920]{1,0:T(8,128)(2,1)S(1)}, bf16[192,1920]{1,0:T(8,128)(2,1)S(1)}, u32[]{:S(2)}, u32[]{:S(2)}) %collective-permute-start.12) | collective-permute-done | bytes 737312 | tf_op jit(solution)/shard_map/ppermute | solution.py:252
  133.7 1.6 collective-permute-start.14
  135.2 5.7 %collective-permute-done.14.refs_4_ = bf16[192,640]{1,0:T(8,128)(2,1)S(1)} collective-permute-done((bf16[192,640]{1,0:T(8,128)(2,1)S(1)}, bf16[192,640]{1,0:T(8,128)(2,1)S(1)}, u32[]{:S(2)}, u32[]{:S(2)}) %collective-permute-start.14) | collective-permute-done | bytes 245792 | tf_op jit(solution)/shard_map/ppermute | solution.py:252
  141.1 1.6 collective-permute-start.15
  142.7 1.5 collective-permute-start.16
  144.3 1.7 step.23
  147.4 1.5 collective-permute-done.16.refs_2_
  149.0 1.7 step.25
  151.4 1.6 collective-permute-start.20
  154.2 4.9 %collective-permute-done.18.refs_4_.refs_5_ = bf16[192,640]{1,0:T(8,128)(2,1)S(1)} collective-permute-done((bf16[192,640]{1,0:T(8,128)(2,1)S(1)}, bf16[192,640]{1,0:T(8,128)(2,1)S(1)}, u32[]{:S(2)}, u32[]{:S(2)}) %collective-permute-start.18) | collective-permute-done | bytes 245792 | tf_op jit(solution)/shard_map/ppermute | solution.py:252
  160.4 1.6 collective-permute-start.22
  162.0 2.8 %collective-permute-done.23.refs_2_ = bf16[192,640]{1,0:T(8,128)(2,1)S(1)} collective-permute-done((bf16[192,640]{1,0:T(8,128)(2,1)S(1)}, bf16[192,640]{1,0:T(8,128)(2,1)S(1)}, u32[]{:S(2)}, u32[]{:S(2)}) %collective-permute-start.23) | collective-permute-done | bytes 245792 | tf_op jit(solution)/shard_map/ppermute | solution.py:252
  164.9 2.0 %collective-permute-done.22.refs_6_ = bf16[192,640]{1,0:T(8,128)(2,1)S(1)} collective-permute-done((bf16[192,640]{1,0:T(8,128)(2,1)S(1)}, bf16[192,640]{1,0:T(8,128)(2,1)S(1)}, u32[]{:S(2)}, u32[]{:S(2)}) %collective-permute-start.22) | collective-permute-done | bytes 245792 | tf_op jit(solution)/shard_map/ppermute | solution.py:252
  (51 shorter events, 13.8 us)
Async XLA Ops:
  6.5 61.8 %all-gather.2.cloned.1.call-start = ((), (), s32[]{:S(2)}) async-start(), calls=%async_computation | async-start | bytes 1310720 | tf_op jit(solution)/shard_map/all_gather | solution.py:529
  6.5 6.6 %copy-start.1 = (bf16[768,256]{1,0:T(8,128)(2,1)S(1)}, bf16[768,256]{1,0:T(8,128)(2,1)}, u32[]{:S(2)}) copy-start(bf16[768,256]{1,0:T(8,128)(2,1)} %keys_hbm.3) | copy-start | bytes 1179652
  6.5 6.6 %copy-start.2 = (bf16[768,256]{1,0:T(8,128)(2,1)S(1)}, bf16[768,256]{1,0:T(8,128)(2,1)}, u32[]{:S(2)}) copy-start(bf16[768,256]{1,0:T(8,128)(2,1)} %values_hbm.3) | copy-start | bytes 1179652
  6.5 6.6 %copy-start.3 = (s32[24,7]{0,1:T(8,128)S(1)}, s32[24,7]{0,1:T(8,128)}, u32[]{:S(2)}) copy-start(s32[24,7]{0,1:T(8,128)} %param.12) | copy-start | bytes 2020
  6.5 6.6 %copy-start.4 = (s32[24]{0:T(128)S(1)}, s32[24]{0:T(128)}, u32[]{:S(2)}) copy-start(s32[24]{0:T(128)} %refs_0_.1) | copy-start | bytes 292
  6.5 6.6 %copy-start.5 = (s32[24]{0:T(128)S(1)}, s32[24]{0:T(128)}, u32[]{:S(2)}) copy-start(s32[24]{0:T(128)} %refs_2_.2) | copy-start | bytes 292
  9.3 55.9 %collective-permute-start = (bf16[640,1280]{1,0:T(8,128)(2,1)}, bf16[640,1280]{1,0:T(8,128)(2,1)S(1)}, u32[]{:S(2)}, u32[]{:S(2)}) collective-permute-start(bf16[640,1280]{1,0:T(8,128)(2,1)} %constant_dynamic-slice_fusion), channel_id=1, source_target_pairs={{0,4},{4,0},{8,12},{12,8},{1,5},{5,1},{9,13},{13,9},{2,6},{6,2},{1... | collective-permute-start | bytes 4915208 | tf_op jit(solution)/shard_map/ppermute | solution.py:405
  12.4 52.9 %collective-permute-start.1 = (bf16[640,1280]{1,0:T(8,128)(2,1)}, bf16[640,1280]{1,0:T(8,128)(2,1)S(1)}, u32[]{:S(2)}, u32[]{:S(2)}) collective-permute-start(bf16[640,1280]{1,0:T(8,128)(2,1)} %constant_dynamic-slice_fusion), channel_id=1, source_target_pairs={{4,8},{8,4},{5,9},{9,5},{6,10},{10,6},{7,11},{11,7},{20,24},{24,20... | collective-permute-start | bytes 4915208 | tf_op jit(solution)/shard_map/ppermute | solution.py:406
  65.2 29.0 %collective-permute-start.2 = (bf16[640,1280]{1,0:T(8,128)(2,1)S(1)}, bf16[640,1280]{1,0:T(8,128)(2,1)}, u32[]{:S(2)}, u32[]{:S(2)}) collective-permute-start(bf16[640,1280]{1,0:T(8,128)(2,1)S(1)} %collective-permute-done.refs_0_.refs_2_), channel_id=1, source_target_pairs={{4,8},{8,4},{5,9},{9,5},{6,10},{10,6},{7,11},{11,7},{20,24},{24,20... | collective-permute-start | bytes 4915208 | tf_op jit(solution)/shard_map/ppermute | solution.py:409
  67.1 42.4 %collective-permute-start.3 = (bf16[640,1280]{1,0:T(8,128)(2,1)S(1)}, bf16[640,1280]{1,0:T(8,128)(2,1)}, u32[]{:S(2)}, u32[]{:S(2)}) collective-permute-start(bf16[640,1280]{1,0:T(8,128)(2,1)S(1)} %collective-permute-done.1.refs_1_.refs_2_), channel_id=1, source_target_pairs={{4,0},{8,12},{5,1},{9,13},{6,2},{10,14},{7,3},{11,15},{20,16},{24,... | collective-permute-start | bytes 4915208 | tf_op jit(solution)/shard_map/ppermute | solution.py:408
  76.7 10.2 %copy-start = (bf16[1280,1280]{1,0:T(8,128)(2,1)S(1)}, bf16[1280,1280]{1,0:T(8,128)(2,1)}, u32[]{:S(2)}) copy-start(bf16[1280,1280]{1,0:T(8,128)(2,1)} %refs_2_.3) | copy-start | bytes 9830404
  76.7 24.8 %collective-permute-start.6 = (bf16[768,640]{1,0:T(8,128)(2,1)S(1)}, bf16[768,640]{1,0:T(8,128)(2,1)S(1)}, u32[]{:S(2)}, u32[]{:S(2)}) collective-permute-start(bf16[768,640]{1,0:T(8,128)(2,1)S(1)} %bitcast.3), channel_id=1, source_target_pairs={{0,16},{16,0},{1,17},{17,1},{2,18},{18,2},{3,19},{19,3},{4,20},{20... | collective-permute-start | bytes 2949128 | tf_op jit(solution)/shard_map/ppermute | solution.py:252
  90.1 1.9 %collective-permute-start.4 = (bf16[384,640]{1,0:T(8,128)(2,1)S(1)}, bf16[384,640]{1,0:T(8,128)(2,1)S(1)}, u32[]{:S(2)}, u32[]{:S(2)}) collective-permute-start(bf16[384,640]{1,0:T(8,128)(2,1)S(1)} %get-tuple-element.37), channel_id=1, source_target_pairs={{0,1},{1,0},{2,3},{3,2},{4,5},{5,4},{6,7},{7,6},{8,9},{9,8},{10,11... | collective-permute-start | bytes 1474568 | tf_op jit(solution)/shard_map/ppermute | solution.py:252
  92.1 11.1 %collective-permute-start.5 = (bf16[192,640]{1,0:T(8,128)(2,1)S(1)}, bf16[192,640]{1,0:T(8,128)(2,1)S(1)}, u32[]{:S(2)}, u32[]{:S(2)}) collective-permute-start(bf16[192,640]{1,0:T(8,128)(2,1)S(1)} %step.16.refs_3_), channel_id=1, source_target_pairs={{0,2},{1,3},{2,0},{3,1},{4,6},{5,7},{6,4},{7,5},{8,10},{9,11},{10,... | collective-permute-start | bytes 737288 | tf_op jit(solution)/shard_map/ppermute | solution.py:252
  93.7 27.1 %collective-permute-start.7 = (bf16[768,640]{1,0:T(8,128)(2,1)S(1)}, bf16[768,640]{1,0:T(8,128)(2,1)S(1)}, u32[]{:S(2)}, u32[]{:S(2)}) collective-permute-start(bf16[768,640]{1,0:T(8,128)(2,1)S(1)} %bitcast.9), channel_id=1, source_target_pairs={{0,16},{16,0},{1,17},{17,1},{2,18},{18,2},{3,19},{19,3},{4,20},{20... | collective-permute-start | bytes 2949128 | tf_op jit(solution)/shard_map/ppermute | solution.py:252
  94.2 50.1 %collective-permute-start.17 = (bf16[640,1280]{1,0:T(8,128)(2,1)}, bf16[640,1280]{1,0:T(8,128)(2,1)S(1)}, u32[]{:S(2)}, u32[]{:S(2)}) collective-permute-start(bf16[640,1280]{1,0:T(8,128)(2,1)} %collective-permute-done.2.refs_2_.refs_3_), channel_id=1, source_target_pairs={{4,0},{8,12},{5,1},{9,13},{6,2},{10,14},{7,3},{11,15},{20,16},{24,... | collective-permute-start | bytes 4915208 | tf_op jit(solution)/shard_map/ppermute | solution.py:446
  101.5 11.2 %collective-permute-start.8 = (bf16[384,640]{1,0:T(8,128)(2,1)S(1)}, bf16[384,640]{1,0:T(8,128)(2,1)S(1)}, u32[]{:S(2)}, u32[]{:S(2)}) collective-permute-start(bf16[384,640]{1,0:T(8,128)(2,1)S(1)} %get-tuple-element.41), channel_id=1, source_target_pairs={{0,1},{1,0},{2,3},{3,2},{4,5},{5,4},{6,7},{7,6},{8,9},{9,8},{10,11... | collective-permute-start | bytes 1474568 | tf_op jit(solution)/shard_map/ppermute | solution.py:252
  103.2 9.5 %collective-permute-start.9 = (bf16[384,640]{1,0:T(8,128)(2,1)S(1)}, bf16[384,640]{1,0:T(8,128)(2,1)S(1)}, u32[]{:S(2)}, u32[]{:S(2)}) collective-permute-start(bf16[384,640]{1,0:T(8,128)(2,1)S(1)} %get-tuple-element.38.refs_7_), channel_id=1, source_target_pairs={{0,1},{1,0},{2,3},{3,2},{4,5},{5,4},{6,7},{7,6},{8,9},{9,8},{10,11... | collective-permute-start | bytes 1474568 | tf_op jit(solution)/shard_map/ppermute | solution.py:252
  112.7 1.9 %collective-permute-start.10 = (bf16[384,640]{1,0:T(8,128)(2,1)S(1)}, bf16[384,640]{1,0:T(8,128)(2,1)S(1)}, u32[]{:S(2)}, u32[]{:S(2)}) collective-permute-start(bf16[384,640]{1,0:T(8,128)(2,1)S(1)} %get-tuple-element.44), channel_id=1, source_target_pairs={{0,1},{1,0},{2,3},{3,2},{4,5},{5,4},{6,7},{7,6},{8,9},{9,8},{10,11... | collective-permute-start | bytes 1474568 | tf_op jit(solution)/shard_map/ppermute | solution.py:252
  114.8 18.6 %collective-permute-start.12 = (bf16[192,1920]{1,0:T(8,128)(2,1)S(1)}, bf16[192,1920]{1,0:T(8,128)(2,1)S(1)}, u32[]{:S(2)}, u32[]{:S(2)}) collective-permute-start(bf16[192,1920]{1,0:T(8,128)(2,1)S(1)} %step.19.refs_5_), channel_id=1, source_target_pairs={{0,2},{1,3},{2,0},{3,1},{4,6},{5,7},{6,4},{7,5},{8,10},{9,11},{10,... | collective-permute-start | bytes 2211848 | tf_op jit(solution)/shard_map/ppermute | solution.py:252
  125.4 1.9 %collective-permute-start.11 = (bf16[384,640]{1,0:T(8,128)(2,1)S(1)}, bf16[384,640]{1,0:T(8,128)(2,1)S(1)}, u32[]{:S(2)}, u32[]{:S(2)}) collective-permute-start(bf16[384,640]{1,0:T(8,128)(2,1)S(1)} %get-tuple-element.46), channel_id=1, source_target_pairs={{0,1},{1,0},{2,3},{3,2},{4,5},{5,4},{6,7},{7,6},{8,9},{9,8},{10,11... | collective-permute-start | bytes 1474568 | tf_op jit(solution)/shard_map/ppermute | solution.py:252
  125.5 9.8 %collective-permute-start.13 = (bf16[384,640]{1,0:T(8,128)(2,1)S(1)}, bf16[384,640]{1,0:T(8,128)(2,1)S(1)}, u32[]{:S(2)}, u32[]{:S(2)}) collective-permute-start(bf16[384,640]{1,0:T(8,128)(2,1)S(1)} %get-tuple-element.51), channel_id=1, source_target_pairs={{0,1},{1,0},{2,3},{3,2},{4,5},{5,4},{6,7},{7,6},{8,9},{9,8},{10,11... | collective-permute-start | bytes 1474568 | tf_op jit(solution)/shard_map/ppermute | solution.py:252
  133.7 7.2 %collective-permute-start.14 = (bf16[192,640]{1,0:T(8,128)(2,1)S(1)}, bf16[192,640]{1,0:T(8,128)(2,1)S(1)}, u32[]{:S(2)}, u32[]{:S(2)}) collective-permute-start(bf16[192,640]{1,0:T(8,128)(2,1)S(1)} %get-tuple-element.52), channel_id=1, source_target_pairs={{0,2},{1,3},{2,0},{3,1},{4,6},{5,7},{6,4},{7,5},{8,10},{9,11},{10,... | collective-permute-start | bytes 737288 | tf_op jit(solution)/shard_map/ppermute | solution.py:252
  141.1 6.3 %collective-permute-start.15 = (bf16[192,640]{1,0:T(8,128)(2,1)S(1)}, bf16[192,640]{1,0:T(8,128)(2,1)S(1)}, u32[]{:S(2)}, u32[]{:S(2)}) collective-permute-start(bf16[192,640]{1,0:T(8,128)(2,1)S(1)} %get-tuple-element.53), channel_id=1, source_target_pairs={{0,16},{16,0},{1,17},{17,1},{2,18},{18,2},{3,19},{19,3},{4,20},{20... | collective-permute-start | bytes 737288 | tf_op jit(solution)/shard_map/ppermute | solution.py:252
  142.7 6.2 %collective-permute-start.16 = (bf16[192,640]{1,0:T(8,128)(2,1)S(1)}, bf16[192,640]{1,0:T(8,128)(2,1)S(1)}, u32[]{:S(2)}, u32[]{:S(2)}) collective-permute-start(bf16[192,640]{1,0:T(8,128)(2,1)S(1)} %get-tuple-element.54.refs_4_), channel_id=1, source_target_pairs={{0,2},{1,3},{2,0},{3,1},{4,6},{5,7},{6,4},{7,5},{8,10},{9,11},{10,... | collective-permute-start | bytes 737288 | tf_op jit(solution)/shard_map/ppermute | solution.py:252
  146.1 5.3 %collective-permute-start.19 = (bf16[384,640]{1,0:T(8,128)(2,1)S(1)}, bf16[384,640]{1,0:T(8,128)(2,1)S(1)}, u32[]{:S(2)}, u32[]{:S(2)}) collective-permute-start(bf16[384,640]{1,0:T(8,128)(2,1)S(1)} %get-tuple-element.55.refs_3_), channel_id=1, source_target_pairs={{0,1},{1,0},{2,3},{3,2},{4,5},{5,4},{6,7},{7,6},{8,9},{9,8},{10,11... | collective-permute-start | bytes 1474568 | tf_op jit(solution)/shard_map/ppermute | solution.py:252
  150.7 2.3 %collective-permute-start.21 = (bf16[384,640]{1,0:T(8,128)(2,1)S(1)}, bf16[384,640]{1,0:T(8,128)(2,1)S(1)}, u32[]{:S(2)}, u32[]{:S(2)}) collective-permute-start(bf16[384,640]{1,0:T(8,128)(2,1)S(1)} %get-tuple-element.57.refs_2_), channel_id=1, source_target_pairs={{0,1},{1,0},{2,3},{3,2},{4,5},{5,4},{6,7},{7,6},{8,9},{9,8},{10,11... | collective-permute-start | bytes 1474568 | tf_op jit(solution)/shard_map/ppermute | solution.py:252
  150.8 8.4 %collective-permute-start.18 = (bf16[192,640]{1,0:T(8,128)(2,1)S(1)}, bf16[192,640]{1,0:T(8,128)(2,1)S(1)}, u32[]{:S(2)}, u32[]{:S(2)}) collective-permute-start(bf16[192,640]{1,0:T(8,128)(2,1)S(1)} %step.24.refs_4_), channel_id=1, source_target_pairs={{0,16},{16,0},{1,17},{17,1},{2,18},{18,2},{3,19},{19,3},{4,20},{20... | collective-permute-start | bytes 737288 | tf_op jit(solution)/shard_map/ppermute | solution.py:252
  151.4 8.9 %collective-permute-start.20 = (bf16[192,640]{1,0:T(8,128)(2,1)S(1)}, bf16[192,640]{1,0:T(8,128)(2,1)S(1)}, u32[]{:S(2)}, u32[]{:S(2)}) collective-permute-start(bf16[192,640]{1,0:T(8,128)(2,1)S(1)} %step.26.refs_2_), channel_id=1, source_target_pairs={{0,2},{1,3},{2,0},{3,1},{4,6},{5,7},{6,4},{7,5},{8,10},{9,11},{10,... | collective-permute-start | bytes 737288 | tf_op jit(solution)/shard_map/ppermute | solution.py:252
  153.0 11.7 %collective-permute-start.23 = (bf16[192,640]{1,0:T(8,128)(2,1)S(1)}, bf16[192,640]{1,0:T(8,128)(2,1)S(1)}, u32[]{:S(2)}, u32[]{:S(2)}) collective-permute-start(bf16[192,640]{1,0:T(8,128)(2,1)S(1)} %step.27.refs_3_), channel_id=1, source_target_pairs={{0,2},{1,3},{2,0},{3,1},{4,6},{5,7},{6,4},{7,5},{8,10},{9,11},{10,... | collective-permute-start | bytes 737288 | tf_op jit(solution)/shard_map/ppermute | solution.py:252
  160.4 6.5 %collective-permute-start.22 = (bf16[192,640]{1,0:T(8,128)(2,1)S(1)}, bf16[192,640]{1,0:T(8,128)(2,1)S(1)}, u32[]{:S(2)}, u32[]{:S(2)}) collective-permute-start(bf16[192,640]{1,0:T(8,128)(2,1)S(1)} %step.28.refs_3_), channel_id=1, source_target_pairs={{0,16},{16,0},{1,17},{17,1},{2,18},{18,2},{3,19},{19,3},{4,20},{20... | collective-permute-start | bytes 737288 | tf_op jit(solution)/shard_map/ppermute | solution.py:252
Sparse Core Ops, SparseCore 0:
  14.9 43.9 all-gather.1
